TPU v7x, 32 devices: a whole 2x2x4 slice. The times are simulated.
32 devices in a mesh: blk: 32 (over z, y, x, core).
Axes of the slice: x: 2, y: 2, z: 4, core: 2. Of those that a mesh axis runs over, the one named last changes fastest.
Arguments:
- populations: float32 [2048, 19, 128], P('blk'), may hold values from 0 to 1, as said below
- relax_rates: float32 [19], replicated, may hold values from 0.6 to 1.8
- destination: int32 [2048], P('blk'), may hold values from 0 to 2559, as said below
- block_links: int32 [2560, 18], P('blk'), may hold values from -1 to 2559, as said below
- site_flags: int32 [2560, 128], P('blk'), may hold values from 0 to 3, as said below
Outputs:
- current: float32 [2560, 19, 128], P('blk')
Inputs may be any that keep to these rules, and one draw needn't show every extreme that they name: `destination`: old positions are in the vessel's geometric order: block g lies in layer g // 16. After the repartition each owner's blocks are consecutive in that order and fill its slots from slot 0 in the same order; only an owner's last blocks leave it, all to the next owner, at most 16 of them; in every draw some owner sends 16 and the next one sends none, so that it holds 80 blocks; every owner holds 48 or more. `block_links`: entry n of an occupied slot's row is the new position of the neighbouring block in direction n, or -1 where the vessel has none; links are mutual; a neighbour lies in the same layer or an adjacent one; rows of empty slots are all -1. `site_flags`: 0 fluid, 1 wall (every site of an empty slot too), 2 inlet, 3 outlet. `populations`: Positive, below the weights times two.
All inputs are finite; a program needn't handle non-finite values.
Results may differ from a plain program's by a relative error of at most 0.0003.
Values sent between devices are 32-bit elements; how exact they have to be, the bound alone decides.
A program may use at most 64 MiB of HBM per device.

v0:
```python
import functools

import jax
import jax.numpy as jnp
import numpy as np
from jax import lax
from jax.experimental import pallas as pl
from jax.experimental.pallas import tpu as pltpu
from jax.sharding import PartitionSpec as P

Q = 19
SITES = 128
LAYER = 16
INLET_SPEED = 0.05
CHUNK = 16
MESH = pl.DeviceIdType.MESH

OFFSETS = [
    (x, y, z)
    for x in (-1, 0, 1)
    for y in (-1, 0, 1)
    for z in (-1, 0, 1)
    if 1 <= abs(x) + abs(y) + abs(z) <= 2
]
VELOCITIES = [(0, 0, 0)] + OFFSETS
WEIGHTS = [(1 / 3, 1 / 18, 1 / 36)[sum(abs(e) for e in c)] for c in VELOCITIES]
INDEX = {c: q for q, c in enumerate(VELOCITIES)}
PAIRS = [q for q in range(10, 19)]


def moment_norms():
    c = np.array(VELOCITIES, np.float64)
    x, y, z = c.T
    e = x * x + y * y + z * z
    f = 5 * e - 9
    s = 3 * e - 5
    xx = 3 * x * x - e
    ww = y * y - z * z
    rows = [
        np.ones(19), 19 * e - 30, (21 * e * e - 53 * e + 24) / 2, x, f * x, y, f * y, z, f * z,
        xx, s * xx, ww, s * ww, x * y, y * z, x * z,
        (y * y - z * z) * x, (z * z - x * x) * y, (x * x - y * y) * z,
    ]
    return [float(np.sum(r * r)) for r in rows]


NORMS = moment_norms()


def regions_of(q):
    cx, cy, cz = VELOCITIES[q]
    found = []
    for nx in sorted({0, -cx}):
        for ny in sorted({0, -cy}):
            for nz in sorted({0, -cz}):
                if (nx, ny, nz) == (0, 0, 0):
                    continue
                shift = (32 * cx + 8 * cy + cz + 32 * ny + 8 * nz) % SITES
                found.append((INDEX[(nx, ny, nz)] - 1, (nx, ny, nz), shift))
    return found


def lane_region(q, step, lane):
    cx, cy, cz = VELOCITIES[q]
    mask = None
    for c, n, value, side in (
        (cx, step[0], lane // 32, 4),
        (cy, step[1], (lane // 8) % 4, 4),
        (cz, step[2], lane % 8, 8),
    ):
        if c == 0:
            continue
        edge = 0 if c > 0 else side - 1
        part = (value == edge) if n != 0 else (value != edge)
        mask = part if mask is None else jnp.logical_and(mask, part)
    return mask


def rolled(value, shift):
    return value if shift % SITES == 0 else pltpu.roll(value, shift % SITES, 1)


def combos(get, jx, jy, jz):
    return {
        (0, 0, 1): jz, (0, 1, 0): jy, (1, 0, 0): jx,
        (0, 1, 1): jy + jz, (0, 1, -1): jy - jz,
        (1, 0, 1): jx + jz, (1, 0, -1): jx - jz,
        (1, 1, 0): jx + jy, (1, -1, 0): jx - jy,
    }


def odd_sums(a):
    x1 = a[(1, 1, 0)] + a[(1, -1, 0)]
    x2 = a[(1, 0, 1)] + a[(1, 0, -1)]
    y1 = a[(1, 1, 0)] - a[(1, -1, 0)]
    y2 = a[(0, 1, 1)] + a[(0, 1, -1)]
    z1 = a[(1, 0, 1)] - a[(1, 0, -1)]
    z2 = a[(0, 1, 1)] - a[(0, 1, -1)]
    return x1, x2, y1, y2, z1, z2


def collide(f, kind, rate):
    pos = [VELOCITIES[q] for q in PAIRS]
    weight = {c: WEIGHTS[INDEX[c]] for c in pos}
    s = {c: f[INDEX[c]] + f[19 - INDEX[c]] for c in pos}
    a = {c: f[INDEX[c]] - f[19 - INDEX[c]] for c in pos}
    density = f[0]
    for c in pos:
        density = density + s[c]
    x1, x2, y1, y2, z1, z2 = odd_sums(a)
    jx = a[(1, 0, 0)] + x1 + x2
    jy = a[(0, 1, 0)] + y1 + y2
    jz = a[(0, 0, 1)] + z1 + z2
    cj = combos(None, jx, jy, jz)
    square = 1.5 * (jx * jx + jy * jy + jz * jz)
    outlet_base = 1.0 - square
    fluid_base = density - square
    quad = {c: 4.5 * (cj[c] * cj[c]) for c in pos}
    d0 = f[0] - WEIGHTS[0] * fluid_base
    ds = {c: s[c] - (2 * weight[c]) * (fluid_base + quad[c]) for c in pos}
    da = {c: a[c] - (6 * weight[c]) * cj[c] for c in pos}
    ax, ay, az = ds[(1, 0, 0)], ds[(0, 1, 0)], ds[(0, 0, 1)]
    dd = ds[(1, 1, 0)] + ds[(1, -1, 0)]
    ee = ds[(1, 0, 1)] + ds[(1, 0, -1)]
    ff = ds[(0, 1, 1)] + ds[(0, 1, -1)]
    s1 = ax + ay + az
    s2 = dd + ee + ff
    p1 = 3.0 * ax - s1
    p2 = s2 - 3.0 * ff
    q1 = ay - az
    q2 = dd - ee
    t0 = rate(0) * (d0 + s1 + s2)
    t1 = rate(1) * (8.0 * s2 - 11.0 * s1 - 30.0 * d0)
    t2 = rate(2) * (12.0 * d0 - 4.0 * s1 + s2)
    t9 = rate(9) * (p1 + p2)
    t10 = rate(10) * (p2 - 2.0 * p1)
    t11 = rate(11) * (q1 + q2)
    t12 = rate(12) * (q2 - 2.0 * q1)
    t13 = rate(13) * (ds[(1, 1, 0)] - ds[(1, -1, 0)])
    t14 = rate(14) * (ds[(0, 1, 1)] - ds[(0, 1, -1)])
    t15 = rate(15) * (ds[(1, 0, 1)] - ds[(1, 0, -1)])
    base1 = t0 - 11.0 * t1 - 4.0 * t2
    base2 = t0 + 8.0 * t1 + t2
    u1 = t9 - 2.0 * t10
    v1 = t11 - 2.0 * t12
    u2 = t9 + t10
    v2 = t11 + t12
    xy, xz, yz = base2 + u2 + v2, base2 + u2 - v2, base2 - 2.0 * u2
    even = {
        (1, 0, 0): base1 + 2.0 * u1, (0, 1, 0): base1 - u1 + v1, (0, 0, 1): base1 - u1 - v1,
        (1, 1, 0): xy + t13, (1, -1, 0): xy - t13,
        (1, 0, 1): xz + t15, (1, 0, -1): xz - t15,
        (0, 1, 1): yz + t14, (0, 1, -1): yz - t14,
    }
    even0 = t0 - 30.0 * t1 + 12.0 * t2
    x1, x2, y1, y2, z1, z2 = odd_sums(da)
    xs, ys, zs = x1 + x2, y1 + y2, z1 + z2
    t3 = rate(3) * (da[(1, 0, 0)] + xs)
    t4 = rate(4) * (xs - 4.0 * da[(1, 0, 0)])
    t5 = rate(5) * (da[(0, 1, 0)] + ys)
    t6 = rate(6) * (ys - 4.0 * da[(0, 1, 0)])
    t7 = rate(7) * (da[(0, 0, 1)] + zs)
    t8 = rate(8) * (zs - 4.0 * da[(0, 0, 1)])
    t16 = rate(16) * (x1 - x2)
    t17 = rate(17) * (y2 - y1)
    t18 = rate(18) * (z1 - z2)
    px, py, pz = t3 + t4, t5 + t6, t7 + t8
    xa, xb = px + t16, px - t16
    ya, yb = py - t17, py + t17
    za, zb = pz + t18, pz - t18
    odd = {
        (1, 0, 0): t3 - 4.0 * t4, (0, 1, 0): t5 - 4.0 * t6, (0, 0, 1): t7 - 4.0 * t8,
        (1, 1, 0): xa + ya, (1, -1, 0): xa - ya,
        (1, 0, 1): xb + za, (1, 0, -1): xb - za,
        (0, 1, 1): yb + zb, (0, 1, -1): yb - zb,
    }
    fluid, wall, inlet = kind == 0, kind == 1, kind == 2
    speed = (0.0, 0.0, INLET_SPEED)
    still = 1.0 - 1.5 * INLET_SPEED**2
    out = [None] * 19
    out[0] = jnp.where(
        fluid, f[0] - even0,
        jnp.where(wall, f[0], jnp.where(inlet, WEIGHTS[0] * still, WEIGHTS[0] * outlet_base)),
    )
    for c in pos:
        dot = sum(p * v for p, v in zip(c, speed))
        half, lean = 0.5 * s[c], 0.5 * a[c]
        ev = jnp.where(
            inlet, weight[c] * (still + 4.5 * dot * dot), weight[c] * (outlet_base + quad[c])
        )
        od = jnp.where(inlet, 3.0 * weight[c] * dot, (3.0 * weight[c]) * cj[c])
        ev = jnp.where(fluid, half - even[c], jnp.where(wall, half, ev))
        od = jnp.where(fluid, lean - odd[c], jnp.where(wall, -lean, od))
        out[INDEX[c]] = ev + od
        out[19 - INDEX[c]] = ev - od
    return out


def kernel(
    n, held, cap, pop_hbm, rates, dest_s, dest_v, flags_v, links_v, out,
    near, low, high, flags_low, flags_high, links_low, links_high, dest_low,
    kinds, reach, hops, split, second, result, send, recv, own_sem,
):
    me = lax.axis_index("blk")
    has_low, has_high = me > 0, me < n - 1
    span_low, span_high = 3 * LAYER, 2 * LAYER
    rows = span_low + held + span_high
    inner = rows - 2 * LAYER
    final = held + LAYER

    barrier = pltpu.get_barrier_semaphore()

    @pl.when(has_high)
    def _():
        pl.semaphore_signal(barrier, inc=1, device_id=(me + 1,), device_id_type=MESH)

    @pl.when(has_low)
    def _():
        pl.semaphore_signal(barrier, inc=1, device_id=(me - 1,), device_id_type=MESH)

    own = pltpu.make_async_copy(pop_hbm, near, own_sem)
    own.start()

    def copy(i, src, dst, target):
        return pltpu.make_async_remote_copy(
            src_ref=src, dst_ref=dst, send_sem=send.at[i], recv_sem=recv.at[i],
            device_id=(target,), device_id_type=MESH,
        )

    up_meta = [
        copy(0, dest_v, dest_low, me + 1),
        copy(1, links_v, links_low, me + 1),
        copy(2, flags_v, flags_low, me + 1),
    ]
    down_meta = [
        copy(3, links_v, links_high, me - 1),
        copy(4, flags_v, flags_high, me - 1),
    ]
    up_pop = copy(5, pop_hbm.at[:, pl.ds(held - span_low, span_low)], low, me + 1)
    down_pop = copy(6, pop_hbm.at[:, pl.ds(0, span_high)], high, me - 1)
    ups, downs = up_meta + [up_pop], down_meta + [down_pop]

    @pl.when(has_low & has_high)
    def _():
        pl.semaphore_wait(barrier, 2)

    @pl.when(jnp.logical_not(has_low & has_high))
    def _():
        pl.semaphore_wait(barrier, 1)

    @pl.when(has_high)
    def _():
        for c in ups:
            c.start()

    @pl.when(has_low)
    def _():
        for c in downs:
            c.start()

    @pl.when(jnp.logical_not(has_low))
    def _():
        low[...] = jnp.zeros_like(low)
        flags_low[...] = jnp.zeros_like(flags_low)
        links_low[...] = jnp.zeros_like(links_low)
        dest_low[...] = jnp.zeros_like(dest_low)

    @pl.when(jnp.logical_not(has_high))
    def _():
        high[...] = jnp.zeros_like(high)
        flags_high[...] = jnp.zeros_like(flags_high)
        links_high[...] = jnp.zeros_like(links_high)

    scale = [rates[k] * (1.0 / NORMS[k]) for k in range(19)]

    def settle(load, kind_at, row, store):
        f = [load(q) for q in range(19)]
        g = collide(f, kind_at, lambda k: scale[k])
        for q in range(19):
            store(q, row, g[q])

    def keep(q, row, value):
        if q > 0:
            high_part = value.astype(jnp.bfloat16)
            low_part = (value - high_part.astype(jnp.float32)).astype(jnp.bfloat16)
            split[q - 1, pl.ds(row, CHUNK), 0:SITES] = high_part
            split[q - 1, pl.ds(row, CHUNK), SITES : 2 * SITES] = low_part

    @pl.when(has_low)
    def _():
        for c in up_meta:
            c.wait_recv()

    @pl.when(has_high)
    def _():
        for c in down_meta:
            c.wait_recv()

    came = dest_v[0:1, 0:1] - me * cap
    came_low = dest_low[0:1, 0:1] - (me - 1) * cap
    gone = jnp.sum(
        jnp.where(dest_v[...] >= (me + 1) * cap, 1.0, 0.0), axis=1, keepdims=True
    ).astype(jnp.int32)

    base_low = held * -1 + span_low - came_low
    base_own = span_low - came
    base_high = span_low + held - gone
    lane_slot = lax.broadcasted_iota(jnp.int32, (1, cap), 1)
    pos_low = base_low + lane_slot
    pos_own = base_own + lane_slot
    pos_high = base_high + lane_slot
    pos_low = jnp.where((pos_low < base_own) & has_low, pos_low, -1)
    pos_own = jnp.where(pos_own < base_high, pos_own, -1)
    pos_high = jnp.where(has_high, pos_high, -1)
    row_id = lax.broadcasted_iota(jnp.int32, (rows, cap), 0)
    picks = [
        jnp.where(row_id == p, 1.0, 0.0).astype(jnp.bfloat16) for p in (pos_low, pos_own, pos_high)
    ]
    total = None
    for pick, ref in zip(picks, (flags_low, flags_v, flags_high)):
        part = jnp.dot(
            pick, ref[...].astype(jnp.float32).astype(jnp.bfloat16),
            preferred_element_type=jnp.float32,
        )
        total = part if total is None else total + part
    kinds[...] = (total + 0.5).astype(jnp.int32)

    total = None
    for pick, ref in zip(picks, (links_low, links_v, links_high)):
        link = ref[...]
        where = jnp.where(
            link >= (me + 1) * cap, base_high + (link - (me + 1) * cap),
            jnp.where(link >= me * cap, base_own + (link - me * cap), base_low + (link - (me - 1) * cap)),
        )
        where = jnp.where((link >= 0) & (where >= 0) & (where < rows), where + 1, 0)
        part = lax.dot_general(
            pick[LAYER : LAYER + inner], where.astype(jnp.float32).astype(jnp.bfloat16),
            (((1,), (1,)), ((), ())), preferred_element_type=jnp.float32,
        )
        total = part if total is None else total + part
    reach[...] = total
    source_id = lax.broadcasted_iota(jnp.int32, (inner, rows), 1).astype(jnp.float32) + 1.0
    for d in range(18):
        column = jnp.broadcast_to(reach[:, d : d + 1], (inner, rows))
        hops[d] = jnp.where(column == source_id, 1.0, 0.0).astype(jnp.bfloat16)

    own.wait()

    def first(ref, base, count):
        def step(i, carry):
            at = pl.multiple_of(i * CHUNK, CHUNK)
            row = pl.multiple_of(base + at, CHUNK)

            def store(q, row, value):
                keep(q, row, value)
                ref[q, pl.ds(at, CHUNK), :] = value

            settle(lambda q: ref[q, pl.ds(at, CHUNK), :], kinds[pl.ds(row, CHUNK), :], row, store)
            return carry

        lax.fori_loop(0, count // CHUNK, step, 0)

    first(near, span_low, held)

    @pl.when(has_low)
    def _():
        up_pop.wait_recv()

    first(low, 0, span_low)

    @pl.when(has_high)
    def _():
        down_pop.wait_recv()

    first(high, span_low + held, span_high)

    def stream(q, own_q, own_opp, lo, count):
        lane = lax.broadcasted_iota(jnp.int32, (count, SITES), 1)
        cx, cy, cz = VELOCITIES[q]
        moved = rolled(own_q, 32 * cx + 8 * cy + cz)
        value = jnp.where(lane_region(q, (0, 0, 0), lane), moved, own_opp)
        entries = regions_of(q)
        picks = [hops[d, lo : lo + count, :] for d, _, _ in entries]
        pick = picks[0] if len(picks) == 1 else jnp.concatenate(picks, axis=0)
        got = jnp.dot(pick, split[q - 1], preferred_element_type=jnp.float32)
        got = got[:, 0:SITES] + got[:, SITES : 2 * SITES]
        for i, (d, step, shift) in enumerate(entries):
            present = jnp.broadcast_to(reach[lo : lo + count, d : d + 1], (count, SITES)) > 0.0
            use = jnp.logical_and(lane_region(q, step, lane), present)
            value = jnp.where(use, rolled(got[i * count : (i + 1) * count], shift), value)
        return value

    def whole(q):
        return jnp.concatenate(
            [low[q, LAYER:span_low, :], near[q], high[q, 0:LAYER, :]], axis=0
        )

    second[0] = whole(0)
    for q in range(1, 19):
        second[q] = stream(q, whole(q), whole(19 - q), 0, inner)

    def again(i, carry):
        at = pl.multiple_of(i * CHUNK, CHUNK)
        row = pl.multiple_of(at + LAYER, CHUNK)

        def store(q, row, value):
            keep(q, row, value)
            second[q, pl.ds(at, CHUNK), :] = value

        settle(lambda q: second[q, pl.ds(at, CHUNK), :], kinds[pl.ds(row, CHUNK), :], row, store)
        return carry

    lax.fori_loop(0, inner // CHUNK, again, 0)

    row_of = lax.broadcasted_iota(jnp.int32, (final, SITES), 0)
    full = row_of < final - gone
    skip = jnp.clip(LAYER - (dest_s[0] - me * cap), 0, LAYER)
    for q in range(19):
        if q == 0:
            value = second[0, LAYER : LAYER + final, :]
        else:
            value = stream(
                q, second[q, LAYER : LAYER + final, :], second[19 - q, LAYER : LAYER + final, :],
                LAYER, final,
            )
        result[q, 0:final, :] = jnp.where(full, value, 0.0)
        result[q, final : final + LAYER, :] = jnp.zeros((LAYER, SITES), jnp.float32)
        out[q] = result[q, pl.ds(skip, cap), :]

    @pl.when(has_high)
    def _():
        for c in ups:
            c.wait_send()

    @pl.when(has_low)
    def _():
        for c in downs:
            c.wait_send()


def local(populations, relax_rates, destination, block_links, site_flags):
    n = lax.axis_size("blk")
    held, cap = populations.shape[0], site_flags.shape[0]
    rows = held + 5 * LAYER
    inner, final = rows - 2 * LAYER, held + LAYER
    vmem = pl.BlockSpec(memory_space=pltpu.VMEM)
    smem = pl.BlockSpec(memory_space=pltpu.SMEM)
    f32, i32 = jnp.float32, jnp.int32
    out = pl.pallas_call(
        functools.partial(kernel, n, held, cap),
        out_shape=jax.ShapeDtypeStruct((Q, cap, SITES), f32),
        in_specs=[pl.BlockSpec(memory_space=pl.ANY), smem, smem, vmem, vmem, vmem],
        out_specs=vmem,
        scratch_shapes=[
            pltpu.VMEM((Q, held, SITES), f32),
            pltpu.VMEM((Q, 3 * LAYER, SITES), f32),
            pltpu.VMEM((Q, 2 * LAYER, SITES), f32),
            pltpu.VMEM((cap, SITES), i32),
            pltpu.VMEM((cap, SITES), i32),
            pltpu.VMEM((18, cap), i32),
            pltpu.VMEM((18, cap), i32),
            pltpu.VMEM((1, held), i32),
            pltpu.VMEM((rows, SITES), i32),
            pltpu.VMEM((inner, 18), f32),
            pltpu.VMEM((18, inner, rows), jnp.bfloat16),
            pltpu.VMEM((18, rows, 2 * SITES), jnp.bfloat16),
            pltpu.VMEM((Q, inner, SITES), f32),
            pltpu.VMEM((Q, final + LAYER, SITES), f32),
            pltpu.SemaphoreType.DMA((7,)),
            pltpu.SemaphoreType.DMA((7,)),
            pltpu.SemaphoreType.DMA,
        ],
        compiler_params=pltpu.CompilerParams(
            collective_id=0, has_side_effects=True, vmem_limit_bytes=48 * 1024 * 1024
        ),
    )(
        jnp.transpose(populations, (1, 0, 2)), relax_rates, destination,
        destination.reshape(1, held), site_flags, jnp.transpose(block_links, (1, 0)),
    )
    return jnp.transpose(out, (1, 0, 2))


def solution(mesh):
    in_specs = (P("blk", None, None), P(), P("blk"), P("blk", None), P("blk", None))
    out_specs = P("blk", None, None)
    return jax.shard_map(local, mesh=mesh, in_specs=in_specs, out_specs=out_specs, check_vma=False)
```

profile of v0, /device:TPU:13, one launch (start us, length us, event | category | flops | bytes accessed | tf_op | source)
XLA Modules:
  0.0 22.1 jit_solution(15643201466528443823)
XLA Ops:
  0.0 0.0 copy-start.3
  0.0 0.0 copy-start.4
  0.0 0.7 %copy-done.3 = s32[64]{0:T(128)S(1)} copy-done((s32[64]{0:T(128)S(1)}, s32[64]{0:T(128)}, u32[]{:S(2)}) %copy-start.3) | copy-done | bytes 280
  0.7 0.0 copy-done.4
  0.7 0.0 copy-start
  0.7 1.1 %copy-done = f32[64,19,128]{2,0,1:T(8,128)S(1)} copy-done((f32[64,19,128]{2,0,1:T(8,128)S(1)}, f32[64,19,128]{2,0,1:T(8,128)}, u32[]{:S(2)}) %copy-start) | copy-done | bytes 622616
  1.7 0.0 copy-start.1
  1.8 0.8 %copy-done.1 = s32[80,128]{1,0:T(8,128)S(1)} copy-done((s32[80,128]{1,0:T(8,128)S(1)}, s32[80,128]{1,0:T(8,128)}, u32[]{:S(2)}) %copy-start.1) | copy-done | bytes 40984
  2.5 0.0 copy-start.2
  2.5 0.7 %copy-done.2 = s32[80,18]{0,1:T(8,128)S(1)} copy-done((s32[80,18]{0,1:T(8,128)S(1)}, s32[80,18]{0,1:T(8,128)}, u32[]{:S(2)}) %copy-start.2) | copy-done | bytes 5784
  3.2 18.0 %shard_map.55 = f32[19,80,128]{2,1,0:T(8,128)S(1)} custom-call(f32[19,64,128]{2,1,0:T(8,128)S(1)} %bitcast.5, f32[19]{0:T(128)S(1)} %copy-done.4, s32[64]{0:T(128)S(1)} %copy-done.3, s32[1,64]{1,0:T(1,128)S(1)} %bitcast.7, s32[80,128]{1,0:T(8,128)S(1)} %copy-done.1, s32[18,80]{1,0:T(8,128)S(1)} %bitcast.6), custom_call_target="tpu_custom_call" | custom-call | tf_op jit(solution)/shard_map/pallas_call | solution.py:449
  21.3 0.9 %copy.7 = f32[80,19,128]{2,0,1:T(8,128)} copy(f32[80,19,128]{2,0,1:T(8,128)S(1)} %bitcast.4) | data formatting | bytes 1556480
Async XLA Ops:
  0.0 0.7 %copy-start.3 = (s32[64]{0:T(128)S(1)}, s32[64]{0:T(128)}, u32[]{:S(2)}) copy-start(s32[64]{0:T(128)} %dest_s.1) | copy-start | bytes 772
  0.0 0.7 %copy-start.4 = (f32[19]{0:T(128)S(1)}, f32[19]{0:T(128)}, u32[]{:S(2)}) copy-start(f32[19]{0:T(128)} %rates.1) | copy-start | bytes 232
  0.7 1.1 %copy-start = (f32[64,19,128]{2,0,1:T(8,128)S(1)}, f32[64,19,128]{2,0,1:T(8,128)}, u32[]{:S(2)}) copy-start(f32[64,19,128]{2,0,1:T(8,128)} %param.5) | copy-start | bytes 1867780
  1.7 0.8 %copy-start.1 = (s32[80,128]{1,0:T(8,128)S(1)}, s32[80,128]{1,0:T(8,128)}, u32[]{:S(2)}) copy-start(s32[80,128]{1,0:T(8,128)} %flags_v.1) | copy-start | bytes 122884
  2.5 0.7 %copy-start.2 = (s32[80,18]{0,1:T(8,128)S(1)}, s32[80,18]{0,1:T(8,128)}, u32[]{:S(2)}) copy-start(s32[80,18]{0,1:T(8,128)} %param.8) | copy-start | bytes 17284
where the time goes:
time: 22.5 us; the launch traced here: 22.1 us
  Pallas kernels  18 us (80%)
  local copies, waits for them, and re-layouts  4.11 us (18%)
    pallas_call x1, Pallas kernels, local(): pl.pallas_call(functools.partial(kernel, n, held, cap), out_shape=jax.Sha...  18 us
    unnamed x11, local copies, waits for them, and re-layouts  4.11 us

commit v1 on v0

--- a/solution.py
+++ b/solution.py
@@ -197,9 +197,10 @@
 
 
 def kernel(
-    n, held, cap, pop_hbm, rates, dest_s, dest_v, flags_v, links_v, out,
+    n, held, cap, pop_hbm, rates_hbm, dest_hbm, flags_hbm, links_hbm, out,
     near, low, high, flags_low, flags_high, links_low, links_high, dest_low,
-    kinds, reach, hops, split, second, result, send, recv, own_sem,
+    kinds, reach, hops, split, second, result, rates, dest_s, dest_v, flags_v, links_v,
+    send, recv, own_sem,
 ):
     me = lax.axis_index("blk")
     has_low, has_high = me > 0, me < n - 1
@@ -218,7 +219,16 @@
     def _():
         pl.semaphore_signal(barrier, inc=1, device_id=(me - 1,), device_id_type=MESH)
 
-    own = pltpu.make_async_copy(pop_hbm, near, own_sem)
+    small = [
+        pltpu.make_async_copy(src, dst, own_sem.at[i])
+        for i, (src, dst) in enumerate((
+            (rates_hbm, rates), (dest_hbm, dest_s), (dest_hbm, dest_v),
+            (flags_hbm, flags_v), (links_hbm, links_v),
+        ))
+    ]
+    for c in small:
+        c.start()
+    own = pltpu.make_async_copy(pop_hbm, near, own_sem.at[5])
     own.start()
 
     def copy(i, src, dst, target):
@@ -228,13 +238,13 @@
         )
 
     up_meta = [
-        copy(0, dest_v, dest_low, me + 1),
-        copy(1, links_v, links_low, me + 1),
-        copy(2, flags_v, flags_low, me + 1),
+        copy(0, dest_hbm, dest_low, me + 1),
+        copy(1, links_hbm, links_low, me + 1),
+        copy(2, flags_hbm, flags_low, me + 1),
     ]
     down_meta = [
-        copy(3, links_v, links_high, me - 1),
-        copy(4, flags_v, flags_high, me - 1),
+        copy(3, links_hbm, links_high, me - 1),
+        copy(4, flags_hbm, flags_high, me - 1),
     ]
     up_pop = copy(5, pop_hbm.at[:, pl.ds(held - span_low, span_low)], low, me + 1)
     down_pop = copy(6, pop_hbm.at[:, pl.ds(0, span_high)], high, me - 1)
@@ -271,7 +281,9 @@
         flags_high[...] = jnp.zeros_like(flags_high)
         links_high[...] = jnp.zeros_like(links_high)
 
-    scale = [rates[k] * (1.0 / NORMS[k]) for k in range(19)]
+    for c in small:
+        c.wait()
+    scale = [rates[0, k] * (1.0 / NORMS[k]) for k in range(19)]
 
     def settle(load, kind_at, row, store):
         f = [load(q) for q in range(19)]
@@ -414,7 +426,7 @@
 
     row_of = lax.broadcasted_iota(jnp.int32, (final, SITES), 0)
     full = row_of < final - gone
-    skip = jnp.clip(LAYER - (dest_s[0] - me * cap), 0, LAYER)
+    skip = jnp.clip(LAYER - (dest_s[0, 0] - me * cap), 0, LAYER)
     for q in range(19):
         if q == 0:
             value = second[0, LAYER : LAYER + final, :]
@@ -444,12 +456,11 @@
     rows = held + 5 * LAYER
     inner, final = rows - 2 * LAYER, held + LAYER
     vmem = pl.BlockSpec(memory_space=pltpu.VMEM)
-    smem = pl.BlockSpec(memory_space=pltpu.SMEM)
     f32, i32 = jnp.float32, jnp.int32
     out = pl.pallas_call(
         functools.partial(kernel, n, held, cap),
         out_shape=jax.ShapeDtypeStruct((Q, cap, SITES), f32),
-        in_specs=[pl.BlockSpec(memory_space=pl.ANY), smem, smem, vmem, vmem, vmem],
+        in_specs=[pl.BlockSpec(memory_space=pl.ANY)] * 5,
         out_specs=vmem,
         scratch_shapes=[
             pltpu.VMEM((Q, held, SITES), f32),
@@ -466,15 +477,20 @@
             pltpu.VMEM((18, rows, 2 * SITES), jnp.bfloat16),
             pltpu.VMEM((Q, inner, SITES), f32),
             pltpu.VMEM((Q, final + LAYER, SITES), f32),
+            pltpu.SMEM((1, 19), f32),
+            pltpu.SMEM((1, held), i32),
+            pltpu.VMEM((1, held), i32),
+            pltpu.VMEM((cap, SITES), i32),
+            pltpu.VMEM((18, cap), i32),
             pltpu.SemaphoreType.DMA((7,)),
             pltpu.SemaphoreType.DMA((7,)),
-            pltpu.SemaphoreType.DMA,
+            pltpu.SemaphoreType.DMA((6,)),
         ],
         compiler_params=pltpu.CompilerParams(
-            collective_id=0, has_side_effects=True, vmem_limit_bytes=48 * 1024 * 1024
+            collective_id=0, has_side_effects=True, vmem_limit_bytes=62 * 1024 * 1024
         ),
     )(
-        jnp.transpose(populations, (1, 0, 2)), relax_rates, destination,
+        jnp.transpose(populations, (1, 0, 2)), relax_rates.reshape(1, Q),
         destination.reshape(1, held), site_flags, jnp.transpose(block_links, (1, 0)),
     )
     return jnp.transpose(out, (1, 0, 2))

time: 22.5 us -> 20.8 us (0.924)
  local copies, waits for them, and re-layouts: 4.11 us -> 2.06 us
  Pallas kernels: 18 us -> 18.5 us
    unnamed x11 -> x1, local copies, waits for them, and re-layouts: 4.11 us -> 2.06 us
    pallas_call x1, Pallas kernels: 18 us -> 18.5 us  [local(): pl.pallas_call(functools.partial(kernel, n, held, cap), out_shape=jax.Sha...]
where the time goes in v1:
time: 20.8 us; the launch traced here: 20.5 us
  Pallas kernels  18.5 us (89%)
  local copies, waits for them, and re-layouts  2.06 us (10%)
    pallas_call x1, Pallas kernels, local(): pl.pallas_call(functools.partial(kernel, n, held, cap), out_shape=jax.Sha...  18.5 us
    unnamed x1, local copies, waits for them, and re-layouts  2.06 us

profile of v1, /device:TPU:13, one launch (start us, length us, event | category | flops | bytes accessed | tf_op | source)
XLA Modules:
  0.0 20.5 jit_solution(4867709953467607893)
XLA Ops:
  0.0 18.5 %shard_map.55 = f32[19,80,128]{2,1,0:T(8,128)} custom-call(f32[19,64,128]{2,1,0:T(8,128)} %bitcast.6, f32[1,19]{1,0:T(1,128)} %bitcast.8, s32[1,64]{1,0:T(1,128)} %bitcast.9, s32[80,128]{1,0:T(8,128)} %flags_hbm.1, s32[18,80]{1,0:T(8,128)} %bitcast.7), custom_call_target="tpu_custom_call" | custom-call | tf_op jit(solution)/shard_map/pallas_call | solution.py:460
  18.5 2.1 %copy.7 = f32[80,19,128]{2,0,1:T(8,128)} copy(f32[80,19,128]{2,0,1:T(8,128)} %bitcast.5) | data formatting | bytes 1556480

commit v2 on v1

--- a/solution.py
+++ b/solution.py
@@ -200,7 +200,7 @@
     n, held, cap, pop_hbm, rates_hbm, dest_hbm, flags_hbm, links_hbm, out,
     near, low, high, flags_low, flags_high, links_low, links_high, dest_low,
     kinds, reach, hops, split, second, result, rates, dest_s, dest_v, flags_v, links_v,
-    send, recv, own_sem,
+    staged, send, recv, own_sem, out_sem,
 ):
     me = lax.axis_index("blk")
     has_low, has_high = me > 0, me < n - 1
@@ -246,9 +246,21 @@
         copy(3, links_hbm, links_high, me - 1),
         copy(4, flags_hbm, flags_high, me - 1),
     ]
-    up_pop = copy(5, pop_hbm.at[:, pl.ds(held - span_low, span_low)], low, me + 1)
-    down_pop = copy(6, pop_hbm.at[:, pl.ds(0, span_high)], high, me - 1)
-    ups, downs = up_meta + [up_pop], down_meta + [down_pop]
+    up_pop = [
+        copy(
+            5 + i, pop_hbm.at[:, pl.ds(held - span_low + i * CHUNK, CHUNK)],
+            low.at[:, pl.ds(i * CHUNK, CHUNK)], me + 1,
+        )
+        for i in range(span_low // CHUNK)
+    ]
+    down_pop = [
+        copy(
+            8 + i, pop_hbm.at[:, pl.ds(i * CHUNK, CHUNK)],
+            high.at[:, pl.ds(i * CHUNK, CHUNK)], me - 1,
+        )
+        for i in range(span_high // CHUNK)
+    ]
+    ups, downs = up_meta + up_pop, down_meta + down_pop
 
     @pl.when(has_low & has_high)
     def _():
@@ -358,9 +370,9 @@
 
     own.wait()
 
-    def first(ref, base, count):
+    def first(ref, base, start, count):
         def step(i, carry):
-            at = pl.multiple_of(i * CHUNK, CHUNK)
+            at = pl.multiple_of(start + i * CHUNK, CHUNK)
             row = pl.multiple_of(base + at, CHUNK)
 
             def store(q, row, value):
@@ -372,19 +384,27 @@
 
         lax.fori_loop(0, count // CHUNK, step, 0)
 
-    first(near, span_low, held)
-
-    @pl.when(has_low)
-    def _():
-        up_pop.wait_recv()
-
-    first(low, 0, span_low)
-
-    @pl.when(has_high)
-    def _():
-        down_pop.wait_recv()
-
-    first(high, span_low + held, span_high)
+    first(near, span_low, 0, held)
+
+    def arrive_low(i):
+        @pl.when(has_low)
+        def _():
+            up_pop[i].wait_recv()
+
+        first(low, 0, i * CHUNK, CHUNK)
+
+    def arrive_high(i):
+        @pl.when(has_high)
+        def _():
+            down_pop[i].wait_recv()
+
+        first(high, span_low + held, i * CHUNK, CHUNK)
+
+    arrive_low(0)
+    arrive_high(0)
+    arrive_low(1)
+    arrive_high(1)
+    arrive_low(2)
 
     def stream(q, own_q, own_opp, lo, count):
         lane = lax.broadcasted_iota(jnp.int32, (count, SITES), 1)
@@ -427,6 +447,7 @@
     row_of = lax.broadcasted_iota(jnp.int32, (final, SITES), 0)
     full = row_of < final - gone
     skip = jnp.clip(LAYER - (dest_s[0, 0] - me * cap), 0, LAYER)
+    leaving = []
     for q in range(19):
         if q == 0:
             value = second[0, LAYER : LAYER + final, :]
@@ -437,7 +458,13 @@
             )
         result[q, 0:final, :] = jnp.where(full, value, 0.0)
         result[q, final : final + LAYER, :] = jnp.zeros((LAYER, SITES), jnp.float32)
-        out[q] = result[q, pl.ds(skip, cap), :]
+        staged[q] = result[q, pl.ds(skip, cap), :]
+        leave = pltpu.make_async_copy(staged.at[q], out.at[q], out_sem.at[q])
+        leave.start()
+        leaving.append(leave)
+
+    for c in leaving:
+        c.wait()
 
     @pl.when(has_high)
     def _():
@@ -455,13 +482,12 @@
     held, cap = populations.shape[0], site_flags.shape[0]
     rows = held + 5 * LAYER
     inner, final = rows - 2 * LAYER, held + LAYER
-    vmem = pl.BlockSpec(memory_space=pltpu.VMEM)
     f32, i32 = jnp.float32, jnp.int32
     out = pl.pallas_call(
         functools.partial(kernel, n, held, cap),
         out_shape=jax.ShapeDtypeStruct((Q, cap, SITES), f32),
         in_specs=[pl.BlockSpec(memory_space=pl.ANY)] * 5,
-        out_specs=vmem,
+        out_specs=pl.BlockSpec(memory_space=pl.ANY),
         scratch_shapes=[
             pltpu.VMEM((Q, held, SITES), f32),
             pltpu.VMEM((Q, 3 * LAYER, SITES), f32),
@@ -482,9 +508,11 @@
             pltpu.VMEM((1, held), i32),
             pltpu.VMEM((cap, SITES), i32),
             pltpu.VMEM((18, cap), i32),
-            pltpu.SemaphoreType.DMA((7,)),
-            pltpu.SemaphoreType.DMA((7,)),
+            pltpu.VMEM((Q, cap, SITES), f32),
+            pltpu.SemaphoreType.DMA((10,)),
+            pltpu.SemaphoreType.DMA((10,)),
             pltpu.SemaphoreType.DMA((6,)),
+            pltpu.SemaphoreType.DMA((Q,)),
         ],
         compiler_params=pltpu.CompilerParams(
             collective_id=0, has_side_effects=True, vmem_limit_bytes=62 * 1024 * 1024

time: 20.8 us -> 20.6 us (level)
  no operation moved by 1% of the time
where the time goes in v2:
time: 20.6 us; the launch traced here: 20.5 us
  Pallas kernels  18.4 us (89%)
  local copies, waits for them, and re-layouts  2.06 us (10%)
    pallas_call x1, Pallas kernels, local(): pl.pallas_call(functools.partial(kernel, n, held, cap), out_shape=jax.Sha...  18.4 us
    unnamed x1, local copies, waits for them, and re-layouts  2.06 us

profile of v2, /device:TPU:13, one launch (start us, length us, event | category | flops | bytes accessed | tf_op | source)
XLA Modules:
  0.0 20.5 jit_solution(14216662374178229560)
XLA Ops:
  0.0 18.4 %shard_map.55 = f32[19,80,128]{2,1,0:T(8,128)} custom-call(f32[19,64,128]{2,1,0:T(8,128)} %bitcast.6, f32[1,19]{1,0:T(1,128)} %bitcast.8, s32[1,64]{1,0:T(1,128)} %bitcast.9, s32[80,128]{1,0:T(8,128)} %flags_hbm.1, s32[18,80]{1,0:T(8,128)} %bitcast.7), custom_call_target="tpu_custom_call" | custom-call | tf_op jit(solution)/shard_map/pallas_call | solution.py:486
  18.4 2.1 %copy.7 = f32[80,19,128]{2,0,1:T(8,128)} copy(f32[80,19,128]{2,0,1:T(8,128)} %bitcast.5) | data formatting | bytes 1556480

commit v3 on v2

--- a/solution.py
+++ b/solution.py
@@ -200,7 +200,7 @@
     n, held, cap, pop_hbm, rates_hbm, dest_hbm, flags_hbm, links_hbm, out,
     near, low, high, flags_low, flags_high, links_low, links_high, dest_low,
     kinds, reach, hops, split, second, result, rates, dest_s, dest_v, flags_v, links_v,
-    staged, send, recv, own_sem, out_sem,
+    send, recv, own_sem,
 ):
     me = lax.axis_index("blk")
     has_low, has_high = me > 0, me < n - 1
@@ -447,7 +447,6 @@
     row_of = lax.broadcasted_iota(jnp.int32, (final, SITES), 0)
     full = row_of < final - gone
     skip = jnp.clip(LAYER - (dest_s[0, 0] - me * cap), 0, LAYER)
-    leaving = []
     for q in range(19):
         if q == 0:
             value = second[0, LAYER : LAYER + final, :]
@@ -458,13 +457,7 @@
             )
         result[q, 0:final, :] = jnp.where(full, value, 0.0)
         result[q, final : final + LAYER, :] = jnp.zeros((LAYER, SITES), jnp.float32)
-        staged[q] = result[q, pl.ds(skip, cap), :]
-        leave = pltpu.make_async_copy(staged.at[q], out.at[q], out_sem.at[q])
-        leave.start()
-        leaving.append(leave)
-
-    for c in leaving:
-        c.wait()
+        out[q] = result[q, pl.ds(skip, cap), :]
 
     @pl.when(has_high)
     def _():
@@ -487,7 +480,7 @@
         functools.partial(kernel, n, held, cap),
         out_shape=jax.ShapeDtypeStruct((Q, cap, SITES), f32),
         in_specs=[pl.BlockSpec(memory_space=pl.ANY)] * 5,
-        out_specs=pl.BlockSpec(memory_space=pl.ANY),
+        out_specs=pl.BlockSpec(memory_space=pltpu.VMEM),
         scratch_shapes=[
             pltpu.VMEM((Q, held, SITES), f32),
             pltpu.VMEM((Q, 3 * LAYER, SITES), f32),
@@ -508,11 +501,9 @@
             pltpu.VMEM((1, held), i32),
             pltpu.VMEM((cap, SITES), i32),
             pltpu.VMEM((18, cap), i32),
-            pltpu.VMEM((Q, cap, SITES), f32),
             pltpu.SemaphoreType.DMA((10,)),
             pltpu.SemaphoreType.DMA((10,)),
             pltpu.SemaphoreType.DMA((6,)),
-            pltpu.SemaphoreType.DMA((Q,)),
         ],
         compiler_params=pltpu.CompilerParams(
             collective_id=0, has_side_effects=True, vmem_limit_bytes=62 * 1024 * 1024

time: 20.6 us -> 20.7 us (level)
  no operation moved by 1% of the time
where the time goes in v3:
time: 20.7 us; the launch traced here: 20.5 us
  Pallas kernels  18.4 us (89%)
  local copies, waits for them, and re-layouts  2.06 us (10%)
    pallas_call x1, Pallas kernels, local(): pl.pallas_call(functools.partial(kernel, n, held, cap), out_shape=jax.Sha...  18.4 us
    unnamed x1, local copies, waits for them, and re-layouts  2.06 us

profile of v3, /device:TPU:13, one launch (start us, length us, event | category | flops | bytes accessed | tf_op | source)
XLA Modules:
  0.0 20.5 jit_solution(1025593395986576051)
XLA Ops:
  0.0 18.4 %shard_map.55 = f32[19,80,128]{2,1,0:T(8,128)} custom-call(f32[19,64,128]{2,1,0:T(8,128)} %bitcast.6, f32[1,19]{1,0:T(1,128)} %bitcast.8, s32[1,64]{1,0:T(1,128)} %bitcast.9, s32[80,128]{1,0:T(8,128)} %flags_hbm.1, s32[18,80]{1,0:T(8,128)} %bitcast.7), custom_call_target="tpu_custom_call" | custom-call | tf_op jit(solution)/shard_map/pallas_call | solution.py:479
  18.5 2.1 %copy.7 = f32[80,19,128]{2,0,1:T(8,128)} copy(f32[80,19,128]{2,0,1:T(8,128)} %bitcast.5) | data formatting | bytes 1556480
